TPU v7x, 256 devices: a whole 4x4x8 slice. The times are simulated.
256 devices in a mesh: target: 8 (over x, core), context: 16 (over z_lo, y), offset: 2 (over z_hi).
Axes of the slice: x: 4, y: 4, z: 8 (z_hi: 2, z_lo: 4; z = z_hi * 4 + z_lo), core: 2. Of those that a mesh axis runs over, the one named last changes fastest.
Arguments:
- tensor: bfloat16 [64, 8192, 2048], P('offset', 'target', 'context'), may hold values from -6 to 6
- context_factor: bfloat16 [2048, 256], P('context'), may hold values from -0.125 to 0.125
- offset_factor: bfloat16 [64, 8], P('offset'), may hold values from -0.75 to 0.75
- target_factor: bfloat16 [8192, 256], P('target'), may hold values from -6 to 6
Outputs:
- new_factor: float32 [8192, 256], P('target')
All inputs are finite; a program needn't handle non-finite values.
Results may differ from a plain program's by a relative error of at most 0.0003.
Values sent between devices are 32-bit elements; how exact they have to be, the bound alone decides.
No kernel may reach another device: no remote copies, remote signals or barrier semaphores. Data moves between devices by JAX's collectives and lax.ppermute only.
A program may use at most 128 MiB of HBM per device.

v0:
```python
import functools

import jax
import jax.numpy as jnp
from jax import lax
from jax.experimental import pallas as pl
from jax.experimental.pallas import tpu as pltpu
from jax.sharding import Mesh
from jax.sharding import PartitionSpec as P

F32, BF16 = jnp.float32, jnp.bfloat16
TARGET = ("x", "core")
GROUP = ("zlo", "y", "zhi")
RING = ("zhi", "zlo")
ROWS_AT_ONCE = 256
NN = (((1,), (0,)), ((), ()))
TN = (((0,), (0,)), ((), ()))
NT = (((1,), (1,)), ((), ()))


def mm(a, b, dims=NN):
    return lax.dot_general(a, b, dims, preferred_element_type=F32)


def halves(value):
    high = value.astype(BF16)
    return high, (value - high.astype(F32)).astype(BF16)


def thirds(value):
    high = value.astype(BF16)
    rest = value - high.astype(F32)
    middle = rest.astype(BF16)
    return high, middle, (rest - middle.astype(F32)).astype(BF16)


def pack_place(x, y, core):
    return (8 * x + 2 * y + core).astype(jnp.int32).reshape(1)


def core_of(place_ref):
    return place_ref[0] & 1


def y_of(place_ref):
    return (place_ref[0] >> 1) & 3


def x_of(place_ref):
    return place_ref[0] >> 3


VMEM_SPEC = pl.BlockSpec(memory_space=pltpu.VMEM)
SMEM_SPEC = pl.BlockSpec(memory_space=pltpu.SMEM)


def in_hbm(value):
    return pltpu.with_memory_space_constraint(value, pltpu.HBM)


def in_vmem(value):
    return pltpu.with_memory_space_constraint(value, pltpu.VMEM)


def call(kernel, out_shape, vmem=16, **more):
    return pl.pallas_call(
        kernel,
        out_shape=out_shape,
        compiler_params=pltpu.CompilerParams(vmem_limit_bytes=vmem * 2**20),
        **more,
    )


def project_kernel(
    place_ref,
    offset_hbm,
    target_hbm,
    tensor_ref,
    high_ref,
    low_hbm,
    own_ref,
    near_ref,
    rest_ref,
    low_ref,
    held_ref,
    offset_ref,
    target_ref,
    factor_ref,
    sems,
):
    offsets, rows, width = tensor_ref.shape
    ranks = offset_ref.shape[0]
    blocks = held_ref.shape[0]
    depth = held_ref.shape[2]
    small = [
        pltpu.make_async_copy(offset_hbm, offset_ref, sems.at[blocks]),
        pltpu.make_async_copy(target_hbm, target_ref, sems.at[blocks + 1]),
    ]
    for copy in small:
        copy.start()
    for block in range(blocks):
        pltpu.make_async_copy(
            tensor_ref.at[:, pl.ds(block * depth, depth), :], held_ref.at[block], sems.at[block]
        ).start()
    for copy in small:
        copy.wait()

    def iota(shape, dim):
        return lax.broadcasted_iota(jnp.int32, shape, dim)

    tall, wide = (ranks * 16, ranks), (offsets, offsets * 16)
    at = iota(tall, 0) // 16
    half = ranks // 2
    core = jnp.where(at >= half, 1 - core_of(place_ref), core_of(place_ref))
    rank_at = 2 * ((at + x_of(place_ref)) % half) + core
    pick = (rank_at == iota(tall, 1)).astype(BF16)
    repeat = (iota(wide, 0) == iota(wide, 1) // 16).astype(BF16)
    spread = mm(mm(pick, offset_ref[...]).astype(BF16), repeat)
    same = iota(spread.shape, 0) % 16 == iota(spread.shape, 1) % 16
    spread = jnp.where(same, spread, 0.0).astype(BF16)
    factor_ref[...] = target_ref[...].astype(F32).T.astype(BF16)

    def contract(block):
        base = block * depth
        for at in range(0, depth, 32):
            sides = [
                held_ref[block, :, at + side : at + side + 16, :].reshape(-1, width) for side in (0, 16)
            ]
            high, low = halves(mm(spread, jnp.concatenate(sides, axis=1)))
            for rank in range(ranks):
                to = slice(rank * width, (rank + 1) * width)
                of = slice(rank * 16, rank * 16 + 16)
                for side in (0, 1):
                    rows_at = slice(base + at + 16 * side, base + at + 16 * side + 16)
                    lanes = slice(side * width, (side + 1) * width)
                    high_ref[rows_at, to] = high[of, lanes]
                    low_ref[rows_at, to] = low[of, lanes]

    def add_product(block):
        here = slice(block * depth, (block + 1) * depth)
        factor = factor_ref[:, here]
        for rank in range(0, ranks, 2):
            to = slice(rank * width, (rank + 2) * width)
            change = mm(factor, high_ref[here, to]) + mm(factor, low_ref[here, to])
            for side in (0, 1):
                part = change[:, side * width : (side + 1) * width]
                out_ref, of = own_ref, rank + side
                if rank >= half:
                    out_ref, of = (near_ref if side else rest_ref), (rank - half) // 2
                out_ref[of] = part if block == 0 else out_ref[of] + part

    def keep(block):
        here = pl.ds(block * depth, depth)
        return pltpu.make_async_copy(low_ref.at[here, :], low_hbm.at[here, :], sems.at[blocks + 2 + block])

    for block in range(blocks):
        pltpu.make_async_copy(
            tensor_ref.at[:, pl.ds(block * depth, depth), :], held_ref.at[block], sems.at[block]
        ).wait()
        contract(block)
        if block > 0:
            add_product(block - 1)
        keep(block).start()
    add_product(blocks - 1)
    for block in range(blocks):
        keep(block).wait()


def project(place, offset, target, tensor):
    offsets, rows, width = tensor.shape
    ranks, columns = offset.shape[1], target.shape[1]
    wide = ranks * width
    blocks = rows // ROWS_AT_ONCE
    return call(
        project_kernel,
        (
            jax.ShapeDtypeStruct((rows, wide), BF16),
            pltpu.HBM((rows, wide), BF16),
        )
        + tuple(jax.ShapeDtypeStruct((n, columns, width), F32) for n in (ranks // 2, ranks // 4, ranks // 4)),
        vmem=24,
        in_specs=[
            SMEM_SPEC,
        ]
        + [pl.BlockSpec(memory_space=pltpu.HBM)] * 3,
        out_specs=(VMEM_SPEC, pl.BlockSpec(memory_space=pltpu.HBM)) + (VMEM_SPEC,) * 3,
        scratch_shapes=[
            pltpu.VMEM((rows, wide), BF16),
            pltpu.VMEM((blocks, offsets, ROWS_AT_ONCE, width), BF16),
            pltpu.VMEM((ranks, offsets), BF16),
            pltpu.VMEM((rows, columns), BF16),
            pltpu.VMEM((columns, rows), BF16),
            pltpu.SemaphoreType.DMA((2 * blocks + 2,)),
        ],
    )(place, in_hbm(offset.T), in_hbm(target), in_hbm(tensor))


def weights_kernel(first_ref, second_ref, third_ref, fourth_ref, context_ref, out_ref):
    total = (first_ref[...] + second_ref[...]) + (third_ref[...] + fourth_ref[...])
    high, low = halves(total)
    context = context_ref[...]
    out_ref[...] = mm(high, context) + mm(low, context)


def sum_and_copy_kernel(parts_ref, out_ref):
    out_ref[...] = jnp.broadcast_to(jnp.sum(parts_ref[...], axis=0)[None], out_ref.shape)


def expand_kernel(weights_ref, context_ref, out_ref):
    high, low = halves(weights_ref[...])
    context = context_ref[...]
    out_ref[...] = mm(context, high, NT) + mm(context, low, NT)


def basis_kernel(high_ref, low_ref, value_ref, out_ref):
    vhigh, vlow = halves(value_ref[...])
    to = slice(0, value_ref.shape[0])
    for at in range(0, out_ref.shape[0], ROWS_AT_ONCE):
        rows = slice(at, at + ROWS_AT_ONCE)
        high = high_ref[rows, to]
        out_ref[rows, :] = mm(high, vhigh) + (mm(high, vlow) + mm(low_ref[rows, to], vhigh))


def rest_kernel(steps, blocks, place_ref, high_ref, low_ref, value_ref, sofar_ref, *out_refs):
    vhigh, vlow = halves(value_ref[...])
    depth = value_ref.shape[0]
    to = slice(depth, 2 * depth)
    for step, out_ref in zip(steps, out_refs):
        count = out_ref.shape[0]
        rows = pl.ds(pl.multiple_of((y_of(place_ref) + step) % blocks * count, count), count)
        high = high_ref[rows, to]
        total = mm(high, vhigh) + (mm(high, vlow) + mm(low_ref[rows, to], vhigh))
        out_ref[...] = sofar_ref[rows, :] + total


def make_basis(place, high, low, own, other, blocks):
    high, low = in_vmem(high), in_vmem(low)
    rows, columns = high.shape[0], own.shape[1]
    part = call(basis_kernel, jax.ShapeDtypeStruct((rows, columns), F32))(high, low, own)
    out = {}
    far = blocks // 2
    for steps in ((far,), tuple(step for step in range(blocks) if step != far)):
        values = call(
            functools.partial(rest_kernel, steps, blocks),
            (jax.ShapeDtypeStruct((rows // blocks, columns), F32),) * len(steps),
            in_specs=[SMEM_SPEC] + [VMEM_SPEC] * 4,
        )(place, high, low, other, part)
        out.update(zip(steps, values))
    return [out[step] for step in range(blocks)]


def gram_kernel(place_ref, basis_ref, out_ref):
    high, low = halves(basis_ref[...])
    cross = mm(high, low, TN)
    gram = mm(high, high, TN) + (cross + cross.T)
    side = gram.shape[0] // 2
    left, middle = gram[side:, :side], side // 2
    shares = [
        jnp.concatenate([gram[:side, :side], left[:middle]], axis=0),
        jnp.concatenate([gram[side:, side:], left[middle:]], axis=0),
    ]
    flip = core_of(place_ref) != 0
    out_ref[0] = jnp.where(flip, shares[1], shares[0])
    out_ref[1] = jnp.where(flip, shares[0], shares[1])


def row(value, at):
    return jnp.broadcast_to(value[at : at + 1, :], value.shape)


def small_inverse(columns):
    left = {(i, k): row(columns[k], i) for k in range(8) for i in range(k, 8)}
    unit, inverse = {}, {}
    for j in range(8):
        root = lax.rsqrt(left[j, j])
        square = root * root
        inverse[j, j] = root
        for k in range(j):
            inverse[j, k] = root * unit[j, k]
        for k in range(j + 1, 8):
            for i in range(k, 8):
                left[i, k] = left[i, k] - (left[i, j] * left[k, j]) * square
        for i in range(j + 1, 8):
            ratio = left[i, j] * square
            for k in range(j):
                unit[i, k] = unit[i, k] - ratio * unit[j, k]
            unit[i, j] = -ratio
    return inverse


def inverse_factor(work_ref):
    size, shape = work_ref.shape[0], (8, 128)
    at_row = lax.broadcasted_iota(jnp.int32, shape, 0)
    for top in range(0, size, 32):
        tiles = list(range(top // 128, size // 128))
        tiles += [size // 128 + t for t in range(top // 128 + 1)]
        rows = [
            {t: work_ref[top + 8 * q : top + 8 * q + 8, 128 * t : 128 * t + 128] for t in tiles}
            for q in range(4)
        ]
        columns = {}
        for q in range(4):
            for k in range(8 * (q + 1)):
                tile, lane = (top + k) // 128, (top + k) % 128
                columns[q, k] = jnp.broadcast_to(rows[q][tile][:, lane : lane + 1], shape)
        for q in range(4):
            inverse = small_inverse([columns[q, 8 * q + k] for k in range(8)])
            factor = {
                (o, j): sum(inverse[j, k] * columns[o, 8 * q + k] for k in range(j + 1))
                for o in range(q + 1, 4)
                for j in range(8)
            }
            for p in range(q + 1, 4):
                for k in range(8):
                    ratios = [row(factor[p, j], k) for j in range(8)]
                    for o in range(p, 4):
                        columns[o, 8 * p + k] -= sum(factor[o, j] * ratios[j] for j in range(8))
            spread = []
            for k in range(8):
                value = jnp.zeros(shape, F32)
                for i in range(k, 8):
                    value = jnp.where(at_row == i, inverse[i, k], value)
                spread.append(value)
            for t in tiles:
                mine = sum(spread[k] * row(rows[q][t], k) for k in range(8))
                rows[q][t] = mine
                for o in range(q + 1, 4):
                    rows[o][t] = rows[o][t] - sum(factor[o, j] * row(mine, j) for j in range(8))
        for q in range(4):
            for t in tiles:
                work_ref[top + 8 * q : top + 8 * q + 8, 128 * t : 128 * t + 128] = rows[q][t]
        below = top + 32
        if below < size:
            done = jnp.concatenate(
                [jnp.concatenate([rows[q][t] for q in range(4)], axis=0) for t in tiles], axis=1
            )
            high, middle, low = thirds(done)
            left = jnp.concatenate([high, high, middle, high, low, middle], axis=0)
            right = jnp.concatenate([high, middle, high, low, high, middle], axis=0)
            start, skip = 128 * tiles[0], below % 128
            change = mm(left[:, below - skip - start : size - start], right, TN)
            for n, t in enumerate(tiles):
                work_ref[below:, 128 * t : 128 * t + 128] -= change[skip:, 128 * n : 128 * n + 128]


def factor_kernel(rows_total, place_ref, own_ref, other_ref, high_ref, low_ref, work_ref):
    size = high_ref.shape[0]
    side = size // 2
    own, other = own_ref[...] / rows_total, other_ref[...] / rows_total
    flip = core_of(place_ref) != 0
    upper, lower = jnp.where(flip, other, own), jnp.where(flip, own, other)
    left = jnp.concatenate([upper[side:], lower[side:]], axis=0)
    work_ref[:side, :side] = upper[:side]
    work_ref[:side, side:size] = left.T
    work_ref[side:, :side] = left
    work_ref[side:, side:size] = lower[:side]
    at_row = lax.broadcasted_iota(jnp.int32, (size, size), 0)
    at_column = lax.broadcasted_iota(jnp.int32, (size, size), 1)
    work_ref[:, size:] = (at_row == at_column).astype(F32)
    inverse_factor(work_ref)
    at_row = lax.broadcasted_iota(jnp.int32, (size, size), 0)
    at_column = lax.broadcasted_iota(jnp.int32, (size, size), 1)
    high_ref[...], low_ref[...] = halves(jnp.where(at_row >= at_column, work_ref[:, size:], 0.0))


def apply_kernel(place_ref, ihigh_ref, ilow_ref, *refs):
    out_hbm, out_ref, sems = refs[-3:]
    parts = refs[:-3]
    ihigh, ilow = ihigh_ref[...], ilow_ref[...]
    writes = []
    for behind, part_ref in enumerate(parts):
        count = part_ref.shape[0]
        high, low = halves(part_ref[...])
        out_ref[behind] = mm(high, ihigh, NT) + (mm(high, ilow, NT) + mm(low, ihigh, NT))
        at = (y_of(place_ref) + len(parts) - behind) % len(parts) * count
        here = pl.ds(pl.multiple_of(at, count), count)
        writes.append(pltpu.make_async_copy(out_ref.at[behind], out_hbm.at[here, :], sems.at[behind]))
        writes[-1].start()
    for write in writes:
        write.wait()


def everyone(value, axes):
    return lax.all_to_all(value, axes, 0, 0)


def ahead(value, axis, steps):
    size = lax.axis_size(axis)
    return lax.ppermute(value, axis, [(at, (at + steps) % size) for at in range(size)])


def gather(value, axis):
    return [value] + [ahead(value, axis, steps) for steps in range(1, lax.axis_size(axis))]


def trade(parts, axis):
    return parts[:1] + [ahead(part, axis, steps) for steps, part in enumerate(parts) if steps]


def swap(value):
    return lax.ppermute(value, "core", [(0, 1), (1, 0)])


def total(values):
    first, second, third, fourth = values
    return (first + third) + (second + fourth)


def invert(place, own, other, columns, rows_total):
    return call(
        functools.partial(factor_kernel, rows_total),
        (jax.ShapeDtypeStruct((columns, columns), BF16),) * 2,
        in_specs=[SMEM_SPEC] + [VMEM_SPEC] * 2,
        scratch_shapes=[pltpu.VMEM((columns, 2 * columns), F32)],
    )(place, own, other)


def finish(place, inverse, blocks):
    count, columns = blocks[0].shape
    number = len(blocks)
    return call(
        apply_kernel,
        jax.ShapeDtypeStruct((number * count, columns), F32),
        in_specs=[SMEM_SPEC] + [VMEM_SPEC] * (2 + number),
        out_specs=pl.BlockSpec(memory_space=pltpu.HBM),
        scratch_shapes=[
            pltpu.VMEM((number, count, columns), F32),
            pltpu.SemaphoreType.DMA((number,)),
        ],
    )(place, *inverse, *blocks)


def on_device(tensor, context, offset, target):
    rows, width = tensor.shape[1:]
    ranks, columns = offset.shape[1], target.shape[1]
    nx, ny, nz = lax.axis_size("x"), lax.axis_size("y"), lax.axis_size(RING)
    place = pack_place(lax.axis_index("x"), lax.axis_index("y"), lax.axis_index("core"))

    high, low, product, near, rest = project(place, offset, target, tensor)

    near, rest = swap(near), swap(rest)
    parts = [product[n] + (near if n % 2 else rest)[n // 2] for n in range(nx)]
    parts = trade(parts, "x")
    part = call(weights_kernel, jax.ShapeDtypeStruct((columns, context.shape[1]), F32))(*parts, context)
    size = ny * nz
    part = everyone(part.reshape(size, columns // size, -1), GROUP)
    part = call(sum_and_copy_kernel, jax.ShapeDtypeStruct(part.shape, F32))(part)
    weights = everyone(part, GROUP).reshape(columns, -1)
    expanded = call(expand_kernel, jax.ShapeDtypeStruct((width, columns), F32))(weights, context)
    behind = gather(expanded, "x")
    own = jnp.concatenate([behind[-n % nx] for n in range(nx)], axis=0)
    basis = make_basis(place, high, low, own, swap(own), ny)

    basis = total(trade(basis, "y"))
    basis = everyone(basis.reshape(nz, rows // ny // nz, columns), RING)
    basis = call(sum_and_copy_kernel, jax.ShapeDtypeStruct(basis.shape, F32))(basis)
    basis = everyone(basis, RING).reshape(rows // ny, columns)

    gram = call(
        gram_kernel,
        jax.ShapeDtypeStruct((2, 3 * columns // 4, columns // 2), F32),
        in_specs=[SMEM_SPEC, VMEM_SPEC],
    )(place, basis)
    mine = total(gather(gram[0] + swap(gram[1]), "y"))
    basis, mine = lax.optimization_barrier((basis, mine))
    blocks = gather(basis, "y")
    mine = total(gather(mine, "x"))
    inverse = invert(place, mine, swap(mine), columns, rows * lax.axis_size(TARGET))
    return finish(place, inverse, blocks)


def solution(mesh):
    fine = Mesh(mesh.devices.reshape(4, 2, 4, 4, 2), ("x", "core") + GROUP)
    placed = (
        P("zhi", TARGET, ("zlo", "y")),
        P(("zlo", "y"), None),
        P("zhi", None),
        P(TARGET, None),
    )
    return jax.shard_map(
        on_device, mesh=fine, in_specs=placed, out_specs=P(TARGET, None), check_vma=False
    )
```

profile of v0, /device:TPU:1, one launch (start us, length us, event | category | flops | bytes accessed | tf_op | source)
XLA Modules:
  0.0 145.6 jit_solution(17265633310783439846)
XLA Ops:
  0.0 5.2 %shard_map.46 = (bf16[1024,1024]{1,0:T(8,128)(2,1)S(1)}, bf16[1024,1024]{1,0:T(8,128)(2,1)}, f32[4,256,128]{2,1,0:T(8,128)S(1)}, f32[2,256,128]{2,1,0:T(8,128)S(1)}, f32[2,256,128]{2,1,0:T(8,128)S(1)}) custom-call(s32[1]{0:T(128)} %bitcast.place_ref, bf16[8,32]{1,0:T(8,128)(2,1)} %bitcast.28, bf16[1024,256]{1,0:T(8,128)(2,1)} %target_hbm.1, ...), custom_call_target="tpu_custom_call" | custom-call | tf_op jit(solution)/shard_map/pallas_call | solution.py:174
  5.3 3.3 %collective-permute-start = (f32[2,256,128]{2,1,0:T(8,128)S(1)}, f32[2,256,128]{2,1,0:T(8,128)S(1)}, u32[]{:S(2)}, u32[]{:S(2)}) collective-permute-start(f32[2,256,128]{2,1,0:T(8,128)S(1)} %get-tuple-element.20), channel_id=1, source_target_pairs={{0,32},{32,0},{1,33},{33,1},{2,34},{34,2},{3,35},{35,3},{4,36},{36... | collective-permute-start | bytes 786440 | tf_op jit(solution)/shard_map/ppermute | solution.py:401
  8.7 1.1 collective-permute-done
  9.7 0.4 collective-permute-done.1
  10.2 0.8 collective-permute-start.4
  11.0 0.7 collective-permute-start.2
  11.7 1.0 collective-permute-start.3
  12.7 2.2 %collective-permute-done.4.fourth_ref = f32[256,128]{1,0:T(8,128)S(1)} collective-permute-done((f32[256,128]{1,0:T(8,128)S(1)}, f32[256,128]{1,0:T(8,128)S(1)}, u32[]{:S(2)}, u32[]{:S(2)}) %collective-permute-start.4) | collective-permute-done | bytes 131104 | tf_op jit(solution)/shard_map/ppermute | solution.py:389
  15.0 2.3 %collective-permute-done.2.second_ref = f32[256,128]{1,0:T(8,128)S(1)} collective-permute-done((f32[256,128]{1,0:T(8,128)S(1)}, f32[256,128]{1,0:T(8,128)S(1)}, u32[]{:S(2)}, u32[]{:S(2)}) %collective-permute-start.2) | collective-permute-done | bytes 131104 | tf_op jit(solution)/shard_map/ppermute | solution.py:389
  17.3 1.4 collective-permute-done.3.third_ref
  18.7 0.2 shard_map.47
  18.9 20.7 %all_to_all.20.parts_ref = f32[32,8,256]{2,1,0:T(8,128)S(1)} all-to-all(f32[32,8,256]{2,1,0:T(8,128)S(1)} %bitcast.26), channel_id=1, replica_groups=mesh['x'=4,'core'=2,'zlo'=4,'y'=4,'zhi'=2] {'zlo','y','zhi'}, dimensions={0} | all-to-all | bytes 524288 | tf_op jit(solution)/shard_map/all_to_all | solution.py:384
  39.7 14.1 %all_to_all.21 = f32[32,8,256]{2,1,0:T(8,128)S(1)} all-to-all(f32[32,8,256]{2,1,0:T(8,128)S(1)} %shard_map.48), channel_id=1, replica_groups=mesh['x'=4,'core'=2,'zlo'=4,'y'=4,'zhi'=2] {'zlo','y','zhi'}, dimensions={0} | all-to-all | bytes 524288 | tf_op jit(solution)/shard_map/all_to_all | solution.py:384
  53.8 0.2 shard_map.49
  54.1 1.4 collective-permute-start.7
  55.5 1.8 %collective-permute-start.6 = (f32[128,256]{1,0:T(8,128)S(1)}, f32[128,256]{1,0:T(8,128)S(1)}, u32[]{:S(2)}, u32[]{:S(2)}) collective-permute-start(f32[128,256]{1,0:T(8,128)S(1)} %shard_map.49), channel_id=1, source_target_pairs={{0,128},{64,192},{128,0},{192,64},{1,129},{65,193},{129,1},{193,65... | collective-permute-start | bytes 393224 | tf_op jit(solution)/shard_map/ppermute | solution.py:389
  57.3 2.0 %collective-permute-start.5 = (f32[128,256]{1,0:T(8,128)S(1)}, f32[128,256]{1,0:T(8,128)S(1)}, u32[]{:S(2)}, u32[]{:S(2)}) collective-permute-start(f32[128,256]{1,0:T(8,128)S(1)} %shard_map.49), channel_id=1, source_target_pairs={{0,192},{64,0},{128,64},{192,128},{1,193},{65,1},{129,65},{193,129... | collective-permute-start | bytes 393224 | tf_op jit(solution)/shard_map/ppermute | solution.py:389
  59.3 1.7 %collective-permute-done.6 = f32[128,256]{1,0:T(8,128)S(1)} collective-permute-done((f32[128,256]{1,0:T(8,128)S(1)}, f32[128,256]{1,0:T(8,128)S(1)}, u32[]{:S(2)}, u32[]{:S(2)}) %collective-permute-start.6) | collective-permute-done | bytes 131104 | tf_op jit(solution)/shard_map/ppermute | solution.py:389
  61.0 0.3 collective-permute-done.5
  61.3 6.4 %collective-permute-start.8 = (f32[512,256]{1,0:T(8,128)S(1)}, f32[512,256]{1,0:T(8,128)S(1)}, u32[]{:S(2)}, u32[]{:S(2)}) collective-permute-start(f32[512,256]{1,0:T(8,128)S(1)} %pad_maximum_fusion.value_ref), channel_id=1, source_target_pairs={{0,32},{32,0},{1,33},{33,1},{2,34},{34,2},{3,35},{35,3},{4,36},{36... | collective-permute-start | bytes 1572872 | tf_op jit(solution)/shard_map/ppermute | solution.py:401
  67.7 1.0 shard_map.50.sofar_ref
  68.7 0.5 collective-permute-done.8.value_ref
  69.3 0.8 shard_map.51
  70.2 2.7 %collective-permute-start.11 = (f32[256,256]{1,0:T(8,128)S(1)}, f32[256,256]{1,0:T(8,128)S(1)}, u32[]{:S(2)}, u32[]{:S(2)}) collective-permute-start(f32[256,256]{1,0:T(8,128)S(1)} %get-tuple-element.24), channel_id=1, source_target_pairs={{0,6},{2,0},{4,2},{6,4},{1,7},{3,1},{5,3},{7,5},{8,14},{10,8},{12,... | collective-permute-start | bytes 786440 | tf_op jit(solution)/shard_map/ppermute | solution.py:389
  72.8 0.4 shard_map.52
  73.2 0.4 collective-permute-start.9
  73.6 5.3 %collective-permute-done.10 = f32[256,256]{1,0:T(8,128)S(1)} collective-permute-done((f32[256,256]{1,0:T(8,128)S(1)}, f32[256,256]{1,0:T(8,128)S(1)}, u32[]{:S(2)}, u32[]{:S(2)}) %collective-permute-start.10) | collective-permute-done | bytes 262176 | tf_op jit(solution)/shard_map/ppermute | solution.py:389
  78.9 5.9 %collective-permute-done.9 = f32[256,256]{1,0:T(8,128)S(1)} collective-permute-done((f32[256,256]{1,0:T(8,128)S(1)}, f32[256,256]{1,0:T(8,128)S(1)}, u32[]{:S(2)}, u32[]{:S(2)}) %collective-permute-start.9) | collective-permute-done | bytes 262176 | tf_op jit(solution)/shard_map/ppermute | solution.py:389
  84.9 12.7 %all_to_all.22.parts_ref = f32[8,32,256]{2,1,0:T(8,128)S(1)} all-to-all(f32[8,32,256]{2,1,0:T(8,128)S(1)} %bitcast.27), channel_id=1, replica_groups=mesh['x'=4,'core'=2,'zlo'=4,'y'=4,'zhi'=2] {'zhi','zlo'}, dimensions={0} | all-to-all | bytes 524288 | tf_op jit(solution)/shard_map/all_to_all | solution.py:384
  97.6 11.9 %all_to_all.23 = f32[8,32,256]{2,1,0:T(8,128)S(1)} all-to-all(f32[8,32,256]{2,1,0:T(8,128)S(1)} %shard_map.53), channel_id=1, replica_groups=mesh['x'=4,'core'=2,'zlo'=4,'y'=4,'zhi'=2] {'zhi','zlo'}, dimensions={0} | all-to-all | bytes 524288 | tf_op jit(solution)/shard_map/all_to_all | solution.py:384
  109.5 0.3 shard_map.54
  109.8 3.7 %collective-permute-start.12 = (f32[192,128]{1,0:T(8,128)S(1)}, f32[192,128]{1,0:T(8,128)S(1)}, u32[]{:S(2)}, u32[]{:S(2)}) collective-permute-start(f32[192,128]{1,0:T(8,128)S(1)} %slice_bitcast_fusion), channel_id=1, source_target_pairs={{0,32},{32,0},{1,33},{33,1},{2,34},{34,2},{3,35},{35,3},{4,36},{36... | collective-permute-start | bytes 294920 | tf_op jit(solution)/shard_map/ppermute | solution.py:401
  113.5 0.9 collective-permute-done.12
  114.5 1.9 %collective-permute-start.15 = (f32[192,128]{1,0:T(8,128)S(1)}, f32[192,128]{1,0:T(8,128)S(1)}, u32[]{:S(2)}, u32[]{:S(2)}) collective-permute-start(f32[192,128]{1,0:T(8,128)S(1)} %fusion.4), channel_id=1, source_target_pairs={{0,6},{2,0},{4,2},{6,4},{1,7},{3,1},{5,3},{7,5},{8,14},{10,8},{12,... | collective-permute-start | bytes 294920 | tf_op jit(solution)/shard_map/ppermute | solution.py:389
  116.4 1.3 collective-permute-start.13
  117.7 0.9 collective-permute-done.15
  118.6 5.2 %collective-permute-done.14 = f32[192,128]{1,0:T(8,128)S(1)} collective-permute-done((f32[192,128]{1,0:T(8,128)S(1)}, f32[192,128]{1,0:T(8,128)S(1)}, u32[]{:S(2)}, u32[]{:S(2)}) %collective-permute-start.14) | collective-permute-done | bytes 98336 | tf_op jit(solution)/shard_map/ppermute | solution.py:389
  123.8 2.5 %collective-permute-start.18 = (f32[192,128]{1,0:T(8,128)S(1)}, f32[192,128]{1,0:T(8,128)S(1)}, u32[]{:S(2)}, u32[]{:S(2)}) collective-permute-start(f32[192,128]{1,0:T(8,128)S(1)} %add_add_fusion.2), channel_id=1, source_target_pairs={{0,192},{64,0},{128,64},{192,128},{1,193},{65,1},{129,65},{193,129... | collective-permute-start | bytes 294920 | tf_op jit(solution)/shard_map/ppermute | solution.py:389
  126.3 1.3 collective-permute-start.16
  127.6 0.2 collective-permute-start.22
  127.8 0.1 collective-permute-done.18
  128.0 1.1 collective-permute-start.20
  129.1 2.7 %collective-permute-done.17 = f32[192,128]{1,0:T(8,128)S(1)} collective-permute-done((f32[192,128]{1,0:T(8,128)S(1)}, f32[192,128]{1,0:T(8,128)S(1)}, u32[]{:S(2)}, u32[]{:S(2)}) %collective-permute-start.17) | collective-permute-done | bytes 98336 | tf_op jit(solution)/shard_map/ppermute | solution.py:389
  131.7 0.8 collective-permute-done.16
  132.6 2.6 %collective-permute-start.19 = (f32[192,128]{1,0:T(8,128)S(1)}, f32[192,128]{1,0:T(8,128)S(1)}, u32[]{:S(2)}, u32[]{:S(2)}) collective-permute-start(f32[192,128]{1,0:T(8,128)S(1)} %add_add_fusion.1.own_ref), channel_id=1, source_target_pairs={{0,32},{32,0},{1,33},{33,1},{2,34},{34,2},{3,35},{35,3},{4,36},{36... | collective-permute-start | bytes 294920 | tf_op jit(solution)/shard_map/ppermute | solution.py:401
  135.2 0.9 collective-permute-done.19.other_ref
  136.1 7.7 %shard_map.55 = (bf16[256,256]{1,0:T(8,128)(2,1)S(1)}, bf16[256,256]{1,0:T(8,128)(2,1)S(1)}) custom-call(s32[1]{0:T(128)} %bitcast.place_ref, f32[192,128]{1,0:T(8,128)S(1)} %add_add_fusion.1.own_ref, f32[192,128]{1,0:T(8,128)S(1)} %collective-permute-done.19.other_ref), custom_call_target="tpu_custom_call" | custom-call | tf_op jit(solution)/shard_map/pallas_call | solution.py:410
  143.9 1.5 %shard_map.56 = f32[1024,256]{1,0:T(8,128)} custom-call(s32[1]{0:T(128)} %bitcast.place_ref, bf16[256,256]{1,0:T(8,128)(2,1)S(1)} %get-tuple-element.26.ihigh_ref, bf16[256,256]{1,0:T(8,128)(2,1)S(1)} %get-tuple-element.27.ilow_ref, f32[256,256]{1,0:T(8,128)S(1)} %bitcast.24, f32[256,256]{1,0:T(8,128)S(1)} %collective-permute-done.20.refs_1_, ...), custom_call_target="tpu_custom_call" | custom-call | tf_op jit(solution)/shard_map/pallas_call | solution.py:421
  (24 shorter events, 0.5 us)
Async XLA Ops:
  0.0 18.7 %copy-start.1 = (bf16[128,256]{1,0:T(8,128)(2,1)S(1)}, bf16[128,256]{1,0:T(8,128)(2,1)}, u32[]{:S(2)}) copy-start(bf16[128,256]{1,0:T(8,128)(2,1)} %context_ref.3) | copy-start | bytes 196612
  5.3 4.5 %collective-permute-start = (f32[2,256,128]{2,1,0:T(8,128)S(1)}, f32[2,256,128]{2,1,0:T(8,128)S(1)}, u32[]{:S(2)}, u32[]{:S(2)}) collective-permute-start(f32[2,256,128]{2,1,0:T(8,128)S(1)} %get-tuple-element.20), channel_id=1, source_target_pairs={{0,32},{32,0},{1,33},{33,1},{2,34},{34,2},{3,35},{35,3},{4,36},{36... | collective-permute-start | bytes 786440 | tf_op jit(solution)/shard_map/ppermute | solution.py:401
  8.6 1.5 %collective-permute-start.1 = (f32[2,256,128]{2,1,0:T(8,128)S(1)}, f32[2,256,128]{2,1,0:T(8,128)S(1)}, u32[]{:S(2)}, u32[]{:S(2)}) collective-permute-start(f32[2,256,128]{2,1,0:T(8,128)S(1)} %get-tuple-element.21), channel_id=1, source_target_pairs={{0,32},{32,0},{1,33},{33,1},{2,34},{34,2},{3,35},{35,3},{4,36},{36... | collective-permute-start | bytes 786440 | tf_op jit(solution)/shard_map/ppermute | solution.py:401
  10.2 57.5 %copy-start = (bf16[1024,1024]{1,0:T(8,128)(2,1)S(1)}, bf16[1024,1024]{1,0:T(8,128)(2,1)}, u32[]{:S(2)}) copy-start(bf16[1024,1024]{1,0:T(8,128)(2,1)} %get-tuple-element.18.low_ref) | copy-start | bytes 6291460
  10.2 4.8 %collective-permute-start.4 = (f32[256,128]{1,0:T(8,128)S(1)}, f32[256,128]{1,0:T(8,128)S(1)}, u32[]{:S(2)}, u32[]{:S(2)}) collective-permute-start(f32[256,128]{1,0:T(8,128)S(1)} %get-tuple-element.29), channel_id=1, source_target_pairs={{0,192},{64,0},{128,64},{192,128},{1,193},{65,1},{129,65},{193,129... | collective-permute-start | bytes 393224 | tf_op jit(solution)/shard_map/ppermute | solution.py:389
  11.0 6.3 %collective-permute-start.2 = (f32[256,128]{1,0:T(8,128)S(1)}, f32[256,128]{1,0:T(8,128)S(1)}, u32[]{:S(2)}, u32[]{:S(2)}) collective-permute-start(f32[256,128]{1,0:T(8,128)S(1)} %get-tuple-element.30), channel_id=1, source_target_pairs={{0,64},{64,128},{128,192},{192,0},{1,65},{65,129},{129,193},{193,1... | collective-permute-start | bytes 393224 | tf_op jit(solution)/shard_map/ppermute | solution.py:389
  11.7 7.0 %collective-permute-start.3 = (f32[256,128]{1,0:T(8,128)S(1)}, f32[256,128]{1,0:T(8,128)S(1)}, u32[]{:S(2)}, u32[]{:S(2)}) collective-permute-start(f32[256,128]{1,0:T(8,128)S(1)} %get-tuple-element.34), channel_id=1, source_target_pairs={{0,128},{64,192},{128,0},{192,64},{1,129},{65,193},{129,1},{193,65... | collective-permute-start | bytes 393224 | tf_op jit(solution)/shard_map/ppermute | solution.py:389
  54.1 5.2 %collective-permute-start.7 = (f32[128,256]{1,0:T(8,128)S(1)}, f32[128,256]{1,0:T(8,128)S(1)}, u32[]{:S(2)}, u32[]{:S(2)}) collective-permute-start(f32[128,256]{1,0:T(8,128)S(1)} %shard_map.49), channel_id=1, source_target_pairs={{0,64},{64,128},{128,192},{192,0},{1,65},{65,129},{129,193},{193,1... | collective-permute-start | bytes 393224 | tf_op jit(solution)/shard_map/ppermute | solution.py:389
  55.5 5.5 %collective-permute-start.6 = (f32[128,256]{1,0:T(8,128)S(1)}, f32[128,256]{1,0:T(8,128)S(1)}, u32[]{:S(2)}, u32[]{:S(2)}) collective-permute-start(f32[128,256]{1,0:T(8,128)S(1)} %shard_map.49), channel_id=1, source_target_pairs={{0,128},{64,192},{128,0},{192,64},{1,129},{65,193},{129,1},{193,65... | collective-permute-start | bytes 393224 | tf_op jit(solution)/shard_map/ppermute | solution.py:389
  57.3 3.9 %collective-permute-start.5 = (f32[128,256]{1,0:T(8,128)S(1)}, f32[128,256]{1,0:T(8,128)S(1)}, u32[]{:S(2)}, u32[]{:S(2)}) collective-permute-start(f32[128,256]{1,0:T(8,128)S(1)} %shard_map.49), channel_id=1, source_target_pairs={{0,192},{64,0},{128,64},{192,128},{1,193},{65,1},{129,65},{193,129... | collective-permute-start | bytes 393224 | tf_op jit(solution)/shard_map/ppermute | solution.py:389
  61.3 8.0 %collective-permute-start.8 = (f32[512,256]{1,0:T(8,128)S(1)}, f32[512,256]{1,0:T(8,128)S(1)}, u32[]{:S(2)}, u32[]{:S(2)}) collective-permute-start(f32[512,256]{1,0:T(8,128)S(1)} %pad_maximum_fusion.value_ref), channel_id=1, source_target_pairs={{0,32},{32,0},{1,33},{33,1},{2,34},{34,2},{3,35},{35,3},{4,36},{36... | collective-permute-start | bytes 1572872 | tf_op jit(solution)/shard_map/ppermute | solution.py:401
  70.1 8.8 %collective-permute-start.10 = (f32[256,256]{1,0:T(8,128)S(1)}, f32[256,256]{1,0:T(8,128)S(1)}, u32[]{:S(2)}, u32[]{:S(2)}) collective-permute-start(f32[256,256]{1,0:T(8,128)S(1)} %get-tuple-element.23), channel_id=1, source_target_pairs={{0,2},{2,4},{4,6},{6,0},{1,3},{3,5},{5,7},{7,1},{8,10},{10,12},{12... | collective-permute-start | bytes 786440 | tf_op jit(solution)/shard_map/ppermute | solution.py:389
  70.2 8.7 %collective-permute-start.11 = (f32[256,256]{1,0:T(8,128)S(1)}, f32[256,256]{1,0:T(8,128)S(1)}, u32[]{:S(2)}, u32[]{:S(2)}) collective-permute-start(f32[256,256]{1,0:T(8,128)S(1)} %get-tuple-element.24), channel_id=1, source_target_pairs={{0,6},{2,0},{4,2},{6,4},{1,7},{3,1},{5,3},{7,5},{8,14},{10,8},{12,... | collective-permute-start | bytes 786440 | tf_op jit(solution)/shard_map/ppermute | solution.py:389
  73.2 11.6 %collective-permute-start.9 = (f32[256,256]{1,0:T(8,128)S(1)}, f32[256,256]{1,0:T(8,128)S(1)}, u32[]{:S(2)}, u32[]{:S(2)}) collective-permute-start(f32[256,256]{1,0:T(8,128)S(1)} %shard_map.52), channel_id=1, source_target_pairs={{0,4},{2,6},{4,0},{6,2},{1,5},{3,7},{5,1},{7,3},{8,12},{10,14},{12... | collective-permute-start | bytes 786440 | tf_op jit(solution)/shard_map/ppermute | solution.py:389
  109.8 4.7 %collective-permute-start.12 = (f32[192,128]{1,0:T(8,128)S(1)}, f32[192,128]{1,0:T(8,128)S(1)}, u32[]{:S(2)}, u32[]{:S(2)}) collective-permute-start(f32[192,128]{1,0:T(8,128)S(1)} %slice_bitcast_fusion), channel_id=1, source_target_pairs={{0,32},{32,0},{1,33},{33,1},{2,34},{34,2},{3,35},{35,3},{4,36},{36... | collective-permute-start | bytes 294920 | tf_op jit(solution)/shard_map/ppermute | solution.py:401
  114.5 4.1 %collective-permute-start.15 = (f32[192,128]{1,0:T(8,128)S(1)}, f32[192,128]{1,0:T(8,128)S(1)}, u32[]{:S(2)}, u32[]{:S(2)}) collective-permute-start(f32[192,128]{1,0:T(8,128)S(1)} %fusion.4), channel_id=1, source_target_pairs={{0,6},{2,0},{4,2},{6,4},{1,7},{3,1},{5,3},{7,5},{8,14},{10,8},{12,... | collective-permute-start | bytes 294920 | tf_op jit(solution)/shard_map/ppermute | solution.py:389
  116.4 7.4 %collective-permute-start.14 = (f32[192,128]{1,0:T(8,128)S(1)}, f32[192,128]{1,0:T(8,128)S(1)}, u32[]{:S(2)}, u32[]{:S(2)}) collective-permute-start(f32[192,128]{1,0:T(8,128)S(1)} %fusion.4), channel_id=1, source_target_pairs={{0,2},{2,4},{4,6},{6,0},{1,3},{3,5},{5,7},{7,1},{8,10},{10,12},{12... | collective-permute-start | bytes 294920 | tf_op jit(solution)/shard_map/ppermute | solution.py:389
  116.4 7.4 %collective-permute-start.13 = (f32[192,128]{1,0:T(8,128)S(1)}, f32[192,128]{1,0:T(8,128)S(1)}, u32[]{:S(2)}, u32[]{:S(2)}) collective-permute-start(f32[192,128]{1,0:T(8,128)S(1)} %fusion.4), channel_id=1, source_target_pairs={{0,4},{2,6},{4,0},{6,2},{1,5},{3,7},{5,1},{7,3},{8,12},{10,14},{12... | collective-permute-start | bytes 294920 | tf_op jit(solution)/shard_map/ppermute | solution.py:389
  123.8 4.1 %collective-permute-start.18 = (f32[192,128]{1,0:T(8,128)S(1)}, f32[192,128]{1,0:T(8,128)S(1)}, u32[]{:S(2)}, u32[]{:S(2)}) collective-permute-start(f32[192,128]{1,0:T(8,128)S(1)} %add_add_fusion.2), channel_id=1, source_target_pairs={{0,192},{64,0},{128,64},{192,128},{1,193},{65,1},{129,65},{193,129... | collective-permute-start | bytes 294920 | tf_op jit(solution)/shard_map/ppermute | solution.py:389
  126.3 5.4 %collective-permute-start.17 = (f32[192,128]{1,0:T(8,128)S(1)}, f32[192,128]{1,0:T(8,128)S(1)}, u32[]{:S(2)}, u32[]{:S(2)}) collective-permute-start(f32[192,128]{1,0:T(8,128)S(1)} %add_add_fusion.2), channel_id=1, source_target_pairs={{0,64},{64,128},{128,192},{192,0},{1,65},{65,129},{129,193},{193,1... | collective-permute-start | bytes 294920 | tf_op jit(solution)/shard_map/ppermute | solution.py:389
  126.3 6.2 %collective-permute-start.16 = (f32[192,128]{1,0:T(8,128)S(1)}, f32[192,128]{1,0:T(8,128)S(1)}, u32[]{:S(2)}, u32[]{:S(2)}) collective-permute-start(f32[192,128]{1,0:T(8,128)S(1)} %add_add_fusion.2), channel_id=1, source_target_pairs={{0,128},{64,192},{128,0},{192,64},{1,129},{65,193},{129,1},{193,65... | collective-permute-start | bytes 294920 | tf_op jit(solution)/shard_map/ppermute | solution.py:389
  127.6 16.3 %collective-permute-start.22 = (f32[256,256]{1,0:T(8,128)S(1)}, f32[256,256]{1,0:T(8,128)S(1)}, u32[]{:S(2)}, u32[]{:S(2)}) collective-permute-start(f32[256,256]{1,0:T(8,128)S(1)} %bitcast.21), channel_id=1, source_target_pairs={{0,6},{2,0},{4,2},{6,4},{1,7},{3,1},{5,3},{7,5},{8,14},{10,8},{12,... | collective-permute-start | bytes 786440 | tf_op jit(solution)/shard_map/ppermute | solution.py:389
  127.8 16.1 %collective-permute-start.21 = (f32[256,256]{1,0:T(8,128)S(1)}, f32[256,256]{1,0:T(8,128)S(1)}, u32[]{:S(2)}, u32[]{:S(2)}) collective-permute-start(f32[256,256]{1,0:T(8,128)S(1)} %bitcast.22), channel_id=1, source_target_pairs={{0,4},{2,6},{4,0},{6,2},{1,5},{3,7},{5,1},{7,3},{8,12},{10,14},{12... | collective-permute-start | bytes 786440 | tf_op jit(solution)/shard_map/ppermute | solution.py:389
  128.0 15.9 %collective-permute-start.20 = (f32[256,256]{1,0:T(8,128)S(1)}, f32[256,256]{1,0:T(8,128)S(1)}, u32[]{:S(2)}, u32[]{:S(2)}) collective-permute-start(f32[256,256]{1,0:T(8,128)S(1)} %bitcast.23), channel_id=1, source_target_pairs={{0,2},{2,4},{4,6},{6,0},{1,3},{3,5},{5,7},{7,1},{8,10},{10,12},{12... | collective-permute-start | bytes 786440 | tf_op jit(solution)/shard_map/ppermute | solution.py:389
  132.6 3.6 %collective-permute-start.19 = (f32[192,128]{1,0:T(8,128)S(1)}, f32[192,128]{1,0:T(8,128)S(1)}, u32[]{:S(2)}, u32[]{:S(2)}) collective-permute-start(f32[192,128]{1,0:T(8,128)S(1)} %add_add_fusion.1.own_ref), channel_id=1, source_target_pairs={{0,32},{32,0},{1,33},{33,1},{2,34},{34,2},{3,35},{35,3},{4,36},{36... | collective-permute-start | bytes 294920 | tf_op jit(solution)/shard_map/ppermute | solution.py:401
where the time goes:
time: 146 us
  blocking collectives  59.4 us (41%)
  starting transfers between devices  35.4 us (24%)
  waiting for transfers between devices  32.8 us (22%)
  Pallas kernels  17.4 us (12%)
    all_to_all x4, blocking collectives, everyone(): return lax.all_to_all(value, axes, 0, 0)  59.4 us
    ppermute x18, waiting for transfers between devices, ahead(): lax.ppermute(value, axis, [(at, (at + steps) % size) for at in range(size)])  28.9 us
    ppermute x18, starting transfers between devices, ahead(): lax.ppermute(value, axis, [(at, (at + steps) % size) for at in range(size)])  19.1 us
    ppermute x5, starting transfers between devices, swap(): return lax.ppermute(value, 'core', [(0, 1), (1, 0)])  16.2 us
    pallas_call x1, Pallas kernels, invert(): call(functools.partial(factor_kernel, rows_total), (jax.ShapeDtypeStruct(...  7.73 us
    pallas_call x1, Pallas kernels, project(): call(project_kernel, (jax.ShapeDtypeStruct((rows, wide), BF16), pltpu.HBM...  5.24 us
    ppermute x5, waiting for transfers between devices, swap(): return lax.ppermute(value, 'core', [(0, 1), (1, 0)])  3.87 us
  transfers between devices with their start and end apart: 23, of which 17 were waited for; matrix products, arithmetic and copies ran while one was open for 0% of the time, Pallas kernels for 6%

commit v1 on v0

--- a/solution.py
+++ b/solution.py
@@ -389,8 +389,16 @@
     return lax.ppermute(value, axis, [(at, (at + steps) % size) for at in range(size)])
 
 
-def gather(value, axis):
-    return [value] + [ahead(value, axis, steps) for steps in range(1, lax.axis_size(axis))]
+def copy_kernel(value_ref, out_ref):
+    out_ref[...] = value_ref[...]
+
+
+def gather(value, axis, late=True):
+    size = lax.axis_size(axis)
+    again = call(copy_kernel, jax.ShapeDtypeStruct(value.shape, F32))(value) if late else value
+    return [value] + [
+        ahead(again if steps == size // 2 else value, axis, steps) for steps in range(1, size)
+    ]
 
 
 def trade(parts, axis):
@@ -463,7 +471,7 @@
     )(place, basis)
     mine = total(gather(gram[0] + swap(gram[1]), "y"))
     basis, mine = lax.optimization_barrier((basis, mine))
-    blocks = gather(basis, "y")
+    blocks = gather(basis, "y", late=False)
     mine = total(gather(mine, "x"))
     inverse = invert(place, mine, swap(mine), columns, rows * lax.axis_size(TARGET))
     return finish(place, inverse, blocks)

time: 146 us -> 145 us (level)
    ppermute x5, starting transfers between devices: 16.2 us -> 14 us  [swap(): return lax.ppermute(value, 'core', [(0, 1), (1, 0)])]
    ppermute x18, starting transfers between devices: 19.1 us -> 21.3 us  [ahead(): lax.ppermute(value, axis, [(at, (at + steps) % size) for at in range(size)])]
  transfers between devices with their start and end apart: 23 -> 23, of which waited for: 17 -> 18; matrix products, arithmetic and copies ran while one was open for 0% -> 0% of each run, Pallas kernels for 6% -> 6%
where the time goes in v1:
time: 145 us
  blocking collectives  59.5 us (41%)
  starting transfers between devices  35.3 us (24%)
  waiting for transfers between devices  32.1 us (22%)
  Pallas kernels  17.5 us (12%)
    all_to_all x4, blocking collectives, everyone(): return lax.all_to_all(value, axes, 0, 0)  59.5 us
    ppermute x18, waiting for transfers between devices, ahead(): lax.ppermute(value, axis, [(at, (at + steps) % size) for at in range(size)])  28.2 us
    ppermute x18, starting transfers between devices, ahead(): lax.ppermute(value, axis, [(at, (at + steps) % size) for at in range(size)])  21.3 us
    ppermute x5, starting transfers between devices, swap(): return lax.ppermute(value, 'core', [(0, 1), (1, 0)])  14 us
    pallas_call x1, Pallas kernels, invert(): call(functools.partial(factor_kernel, rows_total), (jax.ShapeDtypeStruct(...  7.73 us
    pallas_call x1, Pallas kernels, project(): call(project_kernel, (jax.ShapeDtypeStruct((rows, wide), BF16), pltpu.HBM...  5.24 us
    ppermute x5, waiting for transfers between devices, swap(): return lax.ppermute(value, 'core', [(0, 1), (1, 0)])  3.86 us
  transfers between devices with their start and end apart: 23, of which 18 were waited for; matrix products, arithmetic and copies ran while one was open for 0% of the time, Pallas kernels for 6%

profile of v1, /device:TPU:1, one launch (start us, length us, event | category | flops | bytes accessed | tf_op | source)
XLA Modules:
  0.0 144.9 jit_solution(5442669074231532426)
XLA Ops:
  0.0 5.2 %shard_map.46 = (bf16[1024,1024]{1,0:T(8,128)(2,1)S(1)}, bf16[1024,1024]{1,0:T(8,128)(2,1)}, f32[4,256,128]{2,1,0:T(8,128)S(1)}, f32[2,256,128]{2,1,0:T(8,128)S(1)}, f32[2,256,128]{2,1,0:T(8,128)S(1)}) custom-call(s32[1]{0:T(128)} %bitcast.place_ref, bf16[8,32]{1,0:T(8,128)(2,1)} %bitcast.28, bf16[1024,256]{1,0:T(8,128)(2,1)} %target_hbm.1, ...), custom_call_target="tpu_custom_call" | custom-call | tf_op jit(solution)/shard_map/pallas_call | solution.py:174
  5.3 3.3 %collective-permute-start = (f32[2,256,128]{2,1,0:T(8,128)S(1)}, f32[2,256,128]{2,1,0:T(8,128)S(1)}, u32[]{:S(2)}, u32[]{:S(2)}) collective-permute-start(f32[2,256,128]{2,1,0:T(8,128)S(1)} %get-tuple-element.20), channel_id=1, source_target_pairs={{0,32},{32,0},{1,33},{33,1},{2,34},{34,2},{3,35},{35,3},{4,36},{36... | collective-permute-start | bytes 786440 | tf_op jit(solution)/shard_map/ppermute | solution.py:409
  8.7 1.1 collective-permute-done
  9.7 0.4 collective-permute-done.1
  10.2 0.8 collective-permute-start.4
  11.0 0.7 collective-permute-start.2
  11.7 1.0 collective-permute-start.3
  12.7 2.2 %collective-permute-done.4.fourth_ref = f32[256,128]{1,0:T(8,128)S(1)} collective-permute-done((f32[256,128]{1,0:T(8,128)S(1)}, f32[256,128]{1,0:T(8,128)S(1)}, u32[]{:S(2)}, u32[]{:S(2)}) %collective-permute-start.4) | collective-permute-done | bytes 131104 | tf_op jit(solution)/shard_map/ppermute | solution.py:389
  15.0 2.3 %collective-permute-done.2.second_ref = f32[256,128]{1,0:T(8,128)S(1)} collective-permute-done((f32[256,128]{1,0:T(8,128)S(1)}, f32[256,128]{1,0:T(8,128)S(1)}, u32[]{:S(2)}, u32[]{:S(2)}) %collective-permute-start.2) | collective-permute-done | bytes 131104 | tf_op jit(solution)/shard_map/ppermute | solution.py:389
  17.3 1.4 collective-permute-done.3.third_ref
  18.9 20.8 %all_to_all.20.parts_ref = f32[32,8,256]{2,1,0:T(8,128)S(1)} all-to-all(f32[32,8,256]{2,1,0:T(8,128)S(1)} %bitcast.26), channel_id=1, replica_groups=mesh['x'=4,'core'=2,'zlo'=4,'y'=4,'zhi'=2] {'zlo','y','zhi'}, dimensions={0} | all-to-all | bytes 524288 | tf_op jit(solution)/shard_map/all_to_all | solution.py:384
  39.8 14.1 %all_to_all.21 = f32[32,8,256]{2,1,0:T(8,128)S(1)} all-to-all(f32[32,8,256]{2,1,0:T(8,128)S(1)} %shard_map.48), channel_id=1, replica_groups=mesh['x'=4,'core'=2,'zlo'=4,'y'=4,'zhi'=2] {'zlo','y','zhi'}, dimensions={0} | all-to-all | bytes 524288 | tf_op jit(solution)/shard_map/all_to_all | solution.py:384
  54.0 0.2 shard_map.49.value_ref
  54.2 3.2 %collective-permute-start.6 = (f32[128,256]{1,0:T(8,128)S(1)}, f32[128,256]{1,0:T(8,128)S(1)}, u32[]{:S(2)}, u32[]{:S(2)}) collective-permute-start(f32[128,256]{1,0:T(8,128)S(1)} %shard_map.50), channel_id=1, source_target_pairs={{0,128},{64,192},{128,0},{192,64},{1,129},{65,193},{129,1},{193,65... | collective-permute-start | bytes 393224 | tf_op jit(solution)/shard_map/ppermute | solution.py:389
  57.4 2.7 %collective-permute-start.5 = (f32[128,256]{1,0:T(8,128)S(1)}, f32[128,256]{1,0:T(8,128)S(1)}, u32[]{:S(2)}, u32[]{:S(2)}) collective-permute-start(f32[128,256]{1,0:T(8,128)S(1)} %shard_map.49.value_ref), channel_id=1, source_target_pairs={{0,192},{64,0},{128,64},{192,128},{1,193},{65,1},{129,65},{193,129... | collective-permute-start | bytes 393224 | tf_op jit(solution)/shard_map/ppermute | solution.py:389
  60.0 2.3 %collective-permute-done.7 = f32[128,256]{1,0:T(8,128)S(1)} collective-permute-done((f32[128,256]{1,0:T(8,128)S(1)}, f32[128,256]{1,0:T(8,128)S(1)}, u32[]{:S(2)}, u32[]{:S(2)}) %collective-permute-start.7) | collective-permute-done | bytes 131104 | tf_op jit(solution)/shard_map/ppermute | solution.py:389
  62.4 1.0 collective-permute-done.5
  63.4 4.0 %collective-permute-start.8 = (f32[512,256]{1,0:T(8,128)S(1)}, f32[512,256]{1,0:T(8,128)S(1)}, u32[]{:S(2)}, u32[]{:S(2)}) collective-permute-start(f32[512,256]{1,0:T(8,128)S(1)} %pad_maximum_fusion.value_ref), channel_id=1, source_target_pairs={{0,32},{32,0},{1,33},{33,1},{2,34},{34,2},{3,35},{35,3},{4,36},{36... | collective-permute-start | bytes 1572872 | tf_op jit(solution)/shard_map/ppermute | solution.py:409
  67.4 1.0 shard_map.51.sofar_ref
  68.4 0.5 collective-permute-done.8.value_ref
  69.0 0.8 shard_map.52
  69.9 2.7 %collective-permute-start.11 = (f32[256,256]{1,0:T(8,128)S(1)}, f32[256,256]{1,0:T(8,128)S(1)}, u32[]{:S(2)}, u32[]{:S(2)}) collective-permute-start(f32[256,256]{1,0:T(8,128)S(1)} %get-tuple-element.24), channel_id=1, source_target_pairs={{0,6},{2,0},{4,2},{6,4},{1,7},{3,1},{5,3},{7,5},{8,14},{10,8},{12,... | collective-permute-start | bytes 786440 | tf_op jit(solution)/shard_map/ppermute | solution.py:389
  72.5 0.4 shard_map.53
  72.9 0.5 collective-permute-start.9
  73.4 5.2 %collective-permute-done.10 = f32[256,256]{1,0:T(8,128)S(1)} collective-permute-done((f32[256,256]{1,0:T(8,128)S(1)}, f32[256,256]{1,0:T(8,128)S(1)}, u32[]{:S(2)}, u32[]{:S(2)}) %collective-permute-start.10) | collective-permute-done | bytes 262176 | tf_op jit(solution)/shard_map/ppermute | solution.py:389
  78.6 6.0 %collective-permute-done.9 = f32[256,256]{1,0:T(8,128)S(1)} collective-permute-done((f32[256,256]{1,0:T(8,128)S(1)}, f32[256,256]{1,0:T(8,128)S(1)}, u32[]{:S(2)}, u32[]{:S(2)}) %collective-permute-start.9) | collective-permute-done | bytes 262176 | tf_op jit(solution)/shard_map/ppermute | solution.py:389
  84.6 12.6 %all_to_all.22.parts_ref = f32[8,32,256]{2,1,0:T(8,128)S(1)} all-to-all(f32[8,32,256]{2,1,0:T(8,128)S(1)} %bitcast.27), channel_id=1, replica_groups=mesh['x'=4,'core'=2,'zlo'=4,'y'=4,'zhi'=2] {'zhi','zlo'}, dimensions={0} | all-to-all | bytes 524288 | tf_op jit(solution)/shard_map/all_to_all | solution.py:384
  97.3 11.9 %all_to_all.23 = f32[8,32,256]{2,1,0:T(8,128)S(1)} all-to-all(f32[8,32,256]{2,1,0:T(8,128)S(1)} %shard_map.54), channel_id=1, replica_groups=mesh['x'=4,'core'=2,'zlo'=4,'y'=4,'zhi'=2] {'zhi','zlo'}, dimensions={0} | all-to-all | bytes 524288 | tf_op jit(solution)/shard_map/all_to_all | solution.py:384
  109.2 0.3 shard_map.55
  109.5 3.7 %collective-permute-start.12 = (f32[192,128]{1,0:T(8,128)S(1)}, f32[192,128]{1,0:T(8,128)S(1)}, u32[]{:S(2)}, u32[]{:S(2)}) collective-permute-start(f32[192,128]{1,0:T(8,128)S(1)} %slice_bitcast_fusion), channel_id=1, source_target_pairs={{0,32},{32,0},{1,33},{33,1},{2,34},{34,2},{3,35},{35,3},{4,36},{36... | collective-permute-start | bytes 294920 | tf_op jit(solution)/shard_map/ppermute | solution.py:409
  113.3 0.9 collective-permute-done.12
  114.2 0.7 collective-permute-start.13
  114.9 2.4 %collective-permute-start.15 = (f32[192,128]{1,0:T(8,128)S(1)}, f32[192,128]{1,0:T(8,128)S(1)}, u32[]{:S(2)}, u32[]{:S(2)}) collective-permute-start(f32[192,128]{1,0:T(8,128)S(1)} %fusion.4.value_ref), channel_id=1, source_target_pairs={{0,6},{2,0},{4,2},{6,4},{1,7},{3,1},{5,3},{7,5},{8,14},{10,8},{12,... | collective-permute-start | bytes 294920 | tf_op jit(solution)/shard_map/ppermute | solution.py:389
  117.3 2.6 %collective-permute-done.13 = f32[192,128]{1,0:T(8,128)S(1)} collective-permute-done((f32[192,128]{1,0:T(8,128)S(1)}, f32[192,128]{1,0:T(8,128)S(1)}, u32[]{:S(2)}, u32[]{:S(2)}) %collective-permute-start.13) | collective-permute-done | bytes 98336 | tf_op jit(solution)/shard_map/ppermute | solution.py:389
  119.9 1.5 %collective-permute-done.15 = f32[192,128]{1,0:T(8,128)S(1)} collective-permute-done((f32[192,128]{1,0:T(8,128)S(1)}, f32[192,128]{1,0:T(8,128)S(1)}, u32[]{:S(2)}, u32[]{:S(2)}) %collective-permute-start.15) | collective-permute-done | bytes 98336 | tf_op jit(solution)/shard_map/ppermute | solution.py:389
  121.4 0.7 collective-permute-done.14
  122.1 1.5 %collective-permute-start.16 = (f32[192,128]{1,0:T(8,128)S(1)}, f32[192,128]{1,0:T(8,128)S(1)}, u32[]{:S(2)}, u32[]{:S(2)}) collective-permute-start(f32[192,128]{1,0:T(8,128)S(1)} %shard_map.57), channel_id=1, source_target_pairs={{0,128},{64,192},{128,0},{192,64},{1,129},{65,193},{129,1},{193,65... | collective-permute-start | bytes 294920 | tf_op jit(solution)/shard_map/ppermute | solution.py:389
  123.6 1.6 %collective-permute-start.18 = (f32[192,128]{1,0:T(8,128)S(1)}, f32[192,128]{1,0:T(8,128)S(1)}, u32[]{:S(2)}, u32[]{:S(2)}) collective-permute-start(f32[192,128]{1,0:T(8,128)S(1)} %add_add_fusion.2.value_ref), channel_id=1, source_target_pairs={{0,192},{64,0},{128,64},{192,128},{1,193},{65,1},{129,65},{193,129... | collective-permute-start | bytes 294920 | tf_op jit(solution)/shard_map/ppermute | solution.py:389
  125.2 0.5 collective-permute-start.17
  125.7 2.2 %collective-permute-start.22 = (f32[256,256]{1,0:T(8,128)S(1)}, f32[256,256]{1,0:T(8,128)S(1)}, u32[]{:S(2)}, u32[]{:S(2)}) collective-permute-start(f32[256,256]{1,0:T(8,128)S(1)} %bitcast.21), channel_id=1, source_target_pairs={{0,6},{2,0},{4,2},{6,4},{1,7},{3,1},{5,3},{7,5},{8,14},{10,8},{12,... | collective-permute-start | bytes 786440 | tf_op jit(solution)/shard_map/ppermute | solution.py:389
  127.9 0.8 collective-permute-start.21
  128.7 0.4 collective-permute-done.18
  129.1 1.7 %collective-permute-done.17 = f32[192,128]{1,0:T(8,128)S(1)} collective-permute-done((f32[192,128]{1,0:T(8,128)S(1)}, f32[192,128]{1,0:T(8,128)S(1)}, u32[]{:S(2)}, u32[]{:S(2)}) %collective-permute-start.17) | collective-permute-done | bytes 98336 | tf_op jit(solution)/shard_map/ppermute | solution.py:389
  130.9 2.8 %collective-permute-start.19 = (f32[192,128]{1,0:T(8,128)S(1)}, f32[192,128]{1,0:T(8,128)S(1)}, u32[]{:S(2)}, u32[]{:S(2)}) collective-permute-start(f32[192,128]{1,0:T(8,128)S(1)} %add_add_fusion.1.own_ref), channel_id=1, source_target_pairs={{0,32},{32,0},{1,33},{33,1},{2,34},{34,2},{3,35},{35,3},{4,36},{36... | collective-permute-start | bytes 294920 | tf_op jit(solution)/shard_map/ppermute | solution.py:409
  133.7 0.9 collective-permute-done.19.other_ref
  134.6 7.7 %shard_map.58 = (bf16[256,256]{1,0:T(8,128)(2,1)S(1)}, bf16[256,256]{1,0:T(8,128)(2,1)S(1)}) custom-call(s32[1]{0:T(128)} %bitcast.place_ref, f32[192,128]{1,0:T(8,128)S(1)} %add_add_fusion.1.own_ref, f32[192,128]{1,0:T(8,128)S(1)} %collective-permute-done.19.other_ref), custom_call_target="tpu_custom_call" | custom-call | tf_op jit(solution)/shard_map/pallas_call | solution.py:418
  142.4 0.9 collective-permute-done.20.refs_1_
  143.3 1.5 %shard_map.59 = f32[1024,256]{1,0:T(8,128)} custom-call(s32[1]{0:T(128)} %bitcast.place_ref, bf16[256,256]{1,0:T(8,128)(2,1)S(1)} %get-tuple-element.26.ihigh_ref, bf16[256,256]{1,0:T(8,128)(2,1)S(1)} %get-tuple-element.27.ilow_ref, f32[256,256]{1,0:T(8,128)S(1)} %bitcast.24, f32[256,256]{1,0:T(8,128)S(1)} %collective-permute-done.20.refs_1_, ...), custom_call_target="tpu_custom_call" | custom-call | tf_op jit(solution)/shard_map/pallas_call | solution.py:429
  (27 shorter events, 0.8 us)
Async XLA Ops:
  0.0 18.7 %copy-start.1 = (bf16[128,256]{1,0:T(8,128)(2,1)S(1)}, bf16[128,256]{1,0:T(8,128)(2,1)}, u32[]{:S(2)}) copy-start(bf16[128,256]{1,0:T(8,128)(2,1)} %context_ref.3) | copy-start | bytes 196612
  5.3 4.5 %collective-permute-start = (f32[2,256,128]{2,1,0:T(8,128)S(1)}, f32[2,256,128]{2,1,0:T(8,128)S(1)}, u32[]{:S(2)}, u32[]{:S(2)}) collective-permute-start(f32[2,256,128]{2,1,0:T(8,128)S(1)} %get-tuple-element.20), channel_id=1, source_target_pairs={{0,32},{32,0},{1,33},{33,1},{2,34},{34,2},{3,35},{35,3},{4,36},{36... | collective-permute-start | bytes 786440 | tf_op jit(solution)/shard_map/ppermute | solution.py:409
  8.6 1.5 %collective-permute-start.1 = (f32[2,256,128]{2,1,0:T(8,128)S(1)}, f32[2,256,128]{2,1,0:T(8,128)S(1)}, u32[]{:S(2)}, u32[]{:S(2)}) collective-permute-start(f32[2,256,128]{2,1,0:T(8,128)S(1)} %get-tuple-element.21), channel_id=1, source_target_pairs={{0,32},{32,0},{1,33},{33,1},{2,34},{34,2},{3,35},{35,3},{4,36},{36... | collective-permute-start | bytes 786440 | tf_op jit(solution)/shard_map/ppermute | solution.py:409
  10.2 4.8 %collective-permute-start.4 = (f32[256,128]{1,0:T(8,128)S(1)}, f32[256,128]{1,0:T(8,128)S(1)}, u32[]{:S(2)}, u32[]{:S(2)}) collective-permute-start(f32[256,128]{1,0:T(8,128)S(1)} %get-tuple-element.29), channel_id=1, source_target_pairs={{0,192},{64,0},{128,64},{192,128},{1,193},{65,1},{129,65},{193,129... | collective-permute-start | bytes 393224 | tf_op jit(solution)/shard_map/ppermute | solution.py:389
  11.0 6.3 %collective-permute-start.2 = (f32[256,128]{1,0:T(8,128)S(1)}, f32[256,128]{1,0:T(8,128)S(1)}, u32[]{:S(2)}, u32[]{:S(2)}) collective-permute-start(f32[256,128]{1,0:T(8,128)S(1)} %get-tuple-element.30), channel_id=1, source_target_pairs={{0,64},{64,128},{128,192},{192,0},{1,65},{65,129},{129,193},{193,1... | collective-permute-start | bytes 393224 | tf_op jit(solution)/shard_map/ppermute | solution.py:389
  11.7 7.0 %collective-permute-start.3 = (f32[256,128]{1,0:T(8,128)S(1)}, f32[256,128]{1,0:T(8,128)S(1)}, u32[]{:S(2)}, u32[]{:S(2)}) collective-permute-start(f32[256,128]{1,0:T(8,128)S(1)} %get-tuple-element.34), channel_id=1, source_target_pairs={{0,128},{64,192},{128,0},{192,64},{1,129},{65,193},{129,1},{193,65... | collective-permute-start | bytes 393224 | tf_op jit(solution)/shard_map/ppermute | solution.py:389
  18.7 48.7 %copy-start = (bf16[1024,1024]{1,0:T(8,128)(2,1)S(1)}, bf16[1024,1024]{1,0:T(8,128)(2,1)}, u32[]{:S(2)}) copy-start(bf16[1024,1024]{1,0:T(8,128)(2,1)} %get-tuple-element.18.low_ref) | copy-start | bytes 6291460
  54.2 5.8 %collective-permute-start.6 = (f32[128,256]{1,0:T(8,128)S(1)}, f32[128,256]{1,0:T(8,128)S(1)}, u32[]{:S(2)}, u32[]{:S(2)}) collective-permute-start(f32[128,256]{1,0:T(8,128)S(1)} %shard_map.50), channel_id=1, source_target_pairs={{0,128},{64,192},{128,0},{192,64},{1,129},{65,193},{129,1},{193,65... | collective-permute-start | bytes 393224 | tf_op jit(solution)/shard_map/ppermute | solution.py:389
  57.4 5.0 %collective-permute-start.7 = (f32[128,256]{1,0:T(8,128)S(1)}, f32[128,256]{1,0:T(8,128)S(1)}, u32[]{:S(2)}, u32[]{:S(2)}) collective-permute-start(f32[128,256]{1,0:T(8,128)S(1)} %shard_map.49.value_ref), channel_id=1, source_target_pairs={{0,64},{64,128},{128,192},{192,0},{1,65},{65,129},{129,193},{193,1... | collective-permute-start | bytes 393224 | tf_op jit(solution)/shard_map/ppermute | solution.py:389
  57.4 6.0 %collective-permute-start.5 = (f32[128,256]{1,0:T(8,128)S(1)}, f32[128,256]{1,0:T(8,128)S(1)}, u32[]{:S(2)}, u32[]{:S(2)}) collective-permute-start(f32[128,256]{1,0:T(8,128)S(1)} %shard_map.49.value_ref), channel_id=1, source_target_pairs={{0,192},{64,0},{128,64},{192,128},{1,193},{65,1},{129,65},{193,129... | collective-permute-start | bytes 393224 | tf_op jit(solution)/shard_map/ppermute | solution.py:389
  63.4 5.6 %collective-permute-start.8 = (f32[512,256]{1,0:T(8,128)S(1)}, f32[512,256]{1,0:T(8,128)S(1)}, u32[]{:S(2)}, u32[]{:S(2)}) collective-permute-start(f32[512,256]{1,0:T(8,128)S(1)} %pad_maximum_fusion.value_ref), channel_id=1, source_target_pairs={{0,32},{32,0},{1,33},{33,1},{2,34},{34,2},{3,35},{35,3},{4,36},{36... | collective-permute-start | bytes 1572872 | tf_op jit(solution)/shard_map/ppermute | solution.py:409
  69.8 8.8 %collective-permute-start.10 = (f32[256,256]{1,0:T(8,128)S(1)}, f32[256,256]{1,0:T(8,128)S(1)}, u32[]{:S(2)}, u32[]{:S(2)}) collective-permute-start(f32[256,256]{1,0:T(8,128)S(1)} %get-tuple-element.23), channel_id=1, source_target_pairs={{0,2},{2,4},{4,6},{6,0},{1,3},{3,5},{5,7},{7,1},{8,10},{10,12},{12... | collective-permute-start | bytes 786440 | tf_op jit(solution)/shard_map/ppermute | solution.py:389
  69.9 8.7 %collective-permute-start.11 = (f32[256,256]{1,0:T(8,128)S(1)}, f32[256,256]{1,0:T(8,128)S(1)}, u32[]{:S(2)}, u32[]{:S(2)}) collective-permute-start(f32[256,256]{1,0:T(8,128)S(1)} %get-tuple-element.24), channel_id=1, source_target_pairs={{0,6},{2,0},{4,2},{6,4},{1,7},{3,1},{5,3},{7,5},{8,14},{10,8},{12,... | collective-permute-start | bytes 786440 | tf_op jit(solution)/shard_map/ppermute | solution.py:389
  72.9 11.6 %collective-permute-start.9 = (f32[256,256]{1,0:T(8,128)S(1)}, f32[256,256]{1,0:T(8,128)S(1)}, u32[]{:S(2)}, u32[]{:S(2)}) collective-permute-start(f32[256,256]{1,0:T(8,128)S(1)} %shard_map.53), channel_id=1, source_target_pairs={{0,4},{2,6},{4,0},{6,2},{1,5},{3,7},{5,1},{7,3},{8,12},{10,14},{12... | collective-permute-start | bytes 786440 | tf_op jit(solution)/shard_map/ppermute | solution.py:389
  109.5 4.7 %collective-permute-start.12 = (f32[192,128]{1,0:T(8,128)S(1)}, f32[192,128]{1,0:T(8,128)S(1)}, u32[]{:S(2)}, u32[]{:S(2)}) collective-permute-start(f32[192,128]{1,0:T(8,128)S(1)} %slice_bitcast_fusion), channel_id=1, source_target_pairs={{0,32},{32,0},{1,33},{33,1},{2,34},{34,2},{3,35},{35,3},{4,36},{36... | collective-permute-start | bytes 294920 | tf_op jit(solution)/shard_map/ppermute | solution.py:409
  114.2 5.6 %collective-permute-start.13 = (f32[192,128]{1,0:T(8,128)S(1)}, f32[192,128]{1,0:T(8,128)S(1)}, u32[]{:S(2)}, u32[]{:S(2)}) collective-permute-start(f32[192,128]{1,0:T(8,128)S(1)} %shard_map.56), channel_id=1, source_target_pairs={{0,4},{2,6},{4,0},{6,2},{1,5},{3,7},{5,1},{7,3},{8,12},{10,14},{12... | collective-permute-start | bytes 294920 | tf_op jit(solution)/shard_map/ppermute | solution.py:389
  114.9 6.5 %collective-permute-start.15 = (f32[192,128]{1,0:T(8,128)S(1)}, f32[192,128]{1,0:T(8,128)S(1)}, u32[]{:S(2)}, u32[]{:S(2)}) collective-permute-start(f32[192,128]{1,0:T(8,128)S(1)} %fusion.4.value_ref), channel_id=1, source_target_pairs={{0,6},{2,0},{4,2},{6,4},{1,7},{3,1},{5,3},{7,5},{8,14},{10,8},{12,... | collective-permute-start | bytes 294920 | tf_op jit(solution)/shard_map/ppermute | solution.py:389
  117.3 4.7 %collective-permute-start.14 = (f32[192,128]{1,0:T(8,128)S(1)}, f32[192,128]{1,0:T(8,128)S(1)}, u32[]{:S(2)}, u32[]{:S(2)}) collective-permute-start(f32[192,128]{1,0:T(8,128)S(1)} %fusion.4.value_ref), channel_id=1, source_target_pairs={{0,2},{2,4},{4,6},{6,0},{1,3},{3,5},{5,7},{7,1},{8,10},{10,12},{12... | collective-permute-start | bytes 294920 | tf_op jit(solution)/shard_map/ppermute | solution.py:389
  122.1 6.6 %collective-permute-start.16 = (f32[192,128]{1,0:T(8,128)S(1)}, f32[192,128]{1,0:T(8,128)S(1)}, u32[]{:S(2)}, u32[]{:S(2)}) collective-permute-start(f32[192,128]{1,0:T(8,128)S(1)} %shard_map.57), channel_id=1, source_target_pairs={{0,128},{64,192},{128,0},{192,64},{1,129},{65,193},{129,1},{193,65... | collective-permute-start | bytes 294920 | tf_op jit(solution)/shard_map/ppermute | solution.py:389
  123.6 5.5 %collective-permute-start.18 = (f32[192,128]{1,0:T(8,128)S(1)}, f32[192,128]{1,0:T(8,128)S(1)}, u32[]{:S(2)}, u32[]{:S(2)}) collective-permute-start(f32[192,128]{1,0:T(8,128)S(1)} %add_add_fusion.2.value_ref), channel_id=1, source_target_pairs={{0,192},{64,0},{128,64},{192,128},{1,193},{65,1},{129,65},{193,129... | collective-permute-start | bytes 294920 | tf_op jit(solution)/shard_map/ppermute | solution.py:389
  125.2 5.6 %collective-permute-start.17 = (f32[192,128]{1,0:T(8,128)S(1)}, f32[192,128]{1,0:T(8,128)S(1)}, u32[]{:S(2)}, u32[]{:S(2)}) collective-permute-start(f32[192,128]{1,0:T(8,128)S(1)} %add_add_fusion.2.value_ref), channel_id=1, source_target_pairs={{0,64},{64,128},{128,192},{192,0},{1,65},{65,129},{129,193},{193,1... | collective-permute-start | bytes 294920 | tf_op jit(solution)/shard_map/ppermute | solution.py:389
  125.7 16.6 %collective-permute-start.22 = (f32[256,256]{1,0:T(8,128)S(1)}, f32[256,256]{1,0:T(8,128)S(1)}, u32[]{:S(2)}, u32[]{:S(2)}) collective-permute-start(f32[256,256]{1,0:T(8,128)S(1)} %bitcast.21), channel_id=1, source_target_pairs={{0,6},{2,0},{4,2},{6,4},{1,7},{3,1},{5,3},{7,5},{8,14},{10,8},{12,... | collective-permute-start | bytes 786440 | tf_op jit(solution)/shard_map/ppermute | solution.py:389
  127.9 14.4 %collective-permute-start.21 = (f32[256,256]{1,0:T(8,128)S(1)}, f32[256,256]{1,0:T(8,128)S(1)}, u32[]{:S(2)}, u32[]{:S(2)}) collective-permute-start(f32[256,256]{1,0:T(8,128)S(1)} %bitcast.22), channel_id=1, source_target_pairs={{0,4},{2,6},{4,0},{6,2},{1,5},{3,7},{5,1},{7,3},{8,12},{10,14},{12... | collective-permute-start | bytes 786440 | tf_op jit(solution)/shard_map/ppermute | solution.py:389
  128.7 14.6 %collective-permute-start.20 = (f32[256,256]{1,0:T(8,128)S(1)}, f32[256,256]{1,0:T(8,128)S(1)}, u32[]{:S(2)}, u32[]{:S(2)}) collective-permute-start(f32[256,256]{1,0:T(8,128)S(1)} %bitcast.23), channel_id=1, source_target_pairs={{0,2},{2,4},{4,6},{6,0},{1,3},{3,5},{5,7},{7,1},{8,10},{10,12},{12... | collective-permute-start | bytes 786440 | tf_op jit(solution)/shard_map/ppermute | solution.py:389
  130.9 3.7 %collective-permute-start.19 = (f32[192,128]{1,0:T(8,128)S(1)}, f32[192,128]{1,0:T(8,128)S(1)}, u32[]{:S(2)}, u32[]{:S(2)}) collective-permute-start(f32[192,128]{1,0:T(8,128)S(1)} %add_add_fusion.1.own_ref), channel_id=1, source_target_pairs={{0,32},{32,0},{1,33},{33,1},{2,34},{34,2},{3,35},{35,3},{4,36},{36... | collective-permute-start | bytes 294920 | tf_op jit(solution)/shard_map/ppermute | solution.py:409
